TPU v7x, 512 devices: a whole 4x8x8 slice. The times are simulated.
512 devices in a mesh: rep: 8 (over y), head: 64 (over z, x, core).
Axes of the slice: x: 4, y: 8, z: 8, core: 2. Of those that a mesh axis runs over, the one named last changes fastest.
Arguments:
- query: bfloat16 [8, 8192, 8192], P('rep', 'head'), may hold values from -16 to 16
- key: bfloat16 [8, 8192, 1024], P('rep', 'head'), may hold values from -16 to 16
- value: bfloat16 [8, 8192, 1024], P('rep', 'head'), may hold values from -6 to 6
- lengths: int32 [8, 8], P('rep'), may hold values from 1 to 4096, 8192 in all within a row
Outputs:
- attended: bfloat16 [8, 8192, 8192], P('rep', 'head')
Inputs may be any that keep to these rules, and one draw needn't show every extreme that they name: Each slab's 8 lengths sum to 8192, and the longest is exactly 4096.
All inputs are finite; a program needn't handle non-finite values.
Results may differ from a plain program's by a relative error of at most 0.0038.
Values may be sent and summed in bfloat16 or wider, within the bound.
A program may use at most 64 MiB of HBM per device.

v0:
```python
import jax
import jax.numpy as jnp
from jax import lax
from jax.sharding import PartitionSpec as P

Q_HEADS = 64
KV_HEADS = 8
HEAD_DIM = 128


def doc_starts(doc_lengths, count):
    ends = jnp.cumsum(doc_lengths)
    places = jnp.arange(count, dtype=jnp.int32)
    picked = jnp.where(ends[None, :] <= places[:, None], doc_lengths[None, :], 0)
    return jnp.sum(picked, axis=1)


def attend_tile(queries, keys, values, starts, index, tile, offset):
    heads = queries.shape[1]
    q_block = lax.dynamic_slice_in_dim(queries, (index - offset) * tile, tile, 0)
    q_pos = index * tile + jnp.arange(tile, dtype=jnp.int32)
    q_start = lax.dynamic_slice_in_dim(starts, index * tile, tile, 0)
    first = q_start[0] // tile
    scale = float(HEAD_DIM) ** (-0.5)

    def visit(block, carry):
        top, total, accum = carry
        k_block = lax.dynamic_slice_in_dim(keys, (block - offset) * tile, tile, 0)
        v_block = lax.dynamic_slice_in_dim(values, (block - offset) * tile, tile, 0)
        scores = (
            jnp.einsum("qhd,khd->hqk", q_block, k_block, preferred_element_type=jnp.float32) * scale
        )
        k_pos = block * tile + jnp.arange(tile, dtype=jnp.int32)
        allowed = (k_pos[None, :] <= q_pos[:, None]) & (k_pos[None, :] >= q_start[:, None])
        scores = jnp.where(allowed[None], scores, jnp.float32(-1e30))
        new_top = jnp.maximum(top, jnp.max(scores, axis=2))
        weights = jnp.where(allowed[None], jnp.exp(scores - new_top[:, :, None]), jnp.float32(0.0))
        factor = jnp.exp(top - new_top)
        product = jnp.einsum(
            "hqk,khd->hqd",
            weights.astype(jnp.bfloat16),
            v_block,
            preferred_element_type=jnp.float32,
        )
        accum = accum * factor[:, :, None] + product
        total = total * factor + jnp.sum(weights, axis=2)
        return (new_top, total, accum)

    start_state = (
        jnp.full((heads, tile), -1e30, jnp.float32),
        jnp.zeros((heads, tile), jnp.float32),
        jnp.zeros((heads, tile, HEAD_DIM), jnp.float32),
    )
    top, total, accum = lax.fori_loop(first, (index + 1).astype(jnp.int32), visit, start_state)
    result = (accum / total[:, :, None]).astype(jnp.bfloat16)
    return jnp.transpose(result, (1, 0, 2))


def attend_range(queries, keys, values, starts, lower, upper, tile, offset):
    blank = jnp.zeros(queries.shape, jnp.bfloat16)

    def place(index, filled):
        block = attend_tile(queries, keys, values, starts, index, tile, offset)
        return lax.dynamic_update_slice_in_dim(filled, block, (index - offset) * tile, 0)

    return lax.fori_loop(lower, upper, place, blank)


def local(query, key, value, lengths):
    tok_rows = query.shape[1]
    devices = lax.axis_size("head")
    count = tok_rows * devices
    tile = min(512, count)
    ntiles = count // tile
    group = Q_HEADS // KV_HEADS
    q_heads = query.reshape(tok_rows, Q_HEADS, HEAD_DIM)
    k_heads = jnp.repeat(key.reshape(tok_rows, KV_HEADS, HEAD_DIM), group, axis=1)
    v_heads = jnp.repeat(value.reshape(tok_rows, KV_HEADS, HEAD_DIM), group, axis=1)
    queries, keys, values = (
        lax.all_to_all(q_heads, "head", split_axis=1, concat_axis=0, tiled=True),
        lax.all_to_all(k_heads, "head", split_axis=1, concat_axis=0, tiled=True),
        lax.all_to_all(v_heads, "head", split_axis=1, concat_axis=0, tiled=True),
    )
    doc_lengths = lengths[0]
    starts = doc_starts(doc_lengths, count)
    outputs = attend_range(queries, keys, values, starts, jnp.int32(0), jnp.int32(ntiles), tile, 0)
    back = lax.all_to_all(outputs, "head", split_axis=0, concat_axis=1, tiled=True)
    return back.reshape(1, tok_rows, Q_HEADS * HEAD_DIM)


def solution(mesh):
    placed = (
        P("rep", "head", None),
        P("rep", "head", None),
        P("rep", "head", None),
        P("rep", None),
    )
    return jax.shard_map(
        local, mesh=mesh, in_specs=placed, out_specs=P("rep", "head", None), check_vma=False
    )
```

profile of v0, /device:TPU:54, one launch (start us, length us, event | category | flops | bytes accessed | tf_op | source)
XLA Modules:
  0.0 534.2 jit_solution(4896722071673234906)
XLA Ops:
  4.1 13.9 %all-to-all-start = ((bf16[128,64,128]{0,2,1:T(8,128)(2,1)}), bf16[128,64,128]{0,2,1:T(8,128)(2,1)S(1)}, u32[]{:S(2)}, u32[]{:S(2)}) async-start(bf16[128,64,128]{0,2,1:T(8,128)(2,1)} %bitcast.87), calls=%async_computation | async-start | bytes 4194304 | tf_op jit(solution)/shard_map/all_to_all | solution.py:80
  18.1 51.2 %all-to-all-done = bf16[128,64,128]{0,2,1:T(8,128)(2,1)S(1)} async-done(((bf16[128,64,128]{0,2,1:T(8,128)(2,1)}), bf16[128,64,128]{0,2,1:T(8,128)(2,1)S(1)}, u32[]{:S(2)}, u32[]{:S(2)}) %all-to-all-start) | async-done | bytes 2097184 | tf_op jit(solution)/shard_map/all_to_all | solution.py:80
  71.2 5.7 %all-to-all-start.1 = ((bf16[128,64,128]{2,0,1:T(8,128)(2,1)}), bf16[128,64,128]{2,0,1:T(8,128)(2,1)}, u32[]{:S(2)}, u32[]{:S(2)}) async-start(bf16[128,64,128]{2,0,1:T(8,128)(2,1)} %bitcast.86), calls=%async_computation.1 | async-start | bytes 4194304 | tf_op jit(solution)/shard_map/all_to_all | solution.py:81
  77.0 51.1 %all-to-all-done.1 = bf16[128,64,128]{2,0,1:T(8,128)(2,1)} async-done(((bf16[128,64,128]{2,0,1:T(8,128)(2,1)}), bf16[128,64,128]{2,0,1:T(8,128)(2,1)}, u32[]{:S(2)}, u32[]{:S(2)}) %all-to-all-start.1) | async-done | bytes 2097184 | tf_op jit(solution)/shard_map/all_to_all | solution.py:81
  130.0 5.7 %all-to-all-start.2 = ((bf16[128,64,128]{2,0,1:T(8,128)(2,1)}), bf16[128,64,128]{2,0,1:T(8,128)(2,1)}, u32[]{:S(2)}, u32[]{:S(2)}) async-start(bf16[128,64,128]{2,0,1:T(8,128)(2,1)} %bitcast.85), calls=%async_computation.2 | async-start | bytes 4194304 | tf_op jit(solution)/shard_map/all_to_all | solution.py:82
  138.9 48.0 %all-to-all-done.2 = bf16[128,64,128]{2,0,1:T(8,128)(2,1)} async-done(((bf16[128,64,128]{2,0,1:T(8,128)(2,1)}), bf16[128,64,128]{2,0,1:T(8,128)(2,1)}, u32[]{:S(2)}, u32[]{:S(2)}) %all-to-all-start.2) | async-done | bytes 2097184 | tf_op jit(solution)/shard_map/all_to_all | solution.py:82
  187.2 266.7 %while.40 = (s32[]{:T(128)}, bf16[8192,1,128]{2,0,1:T(8,128)(2,1)S(1)}, s32[8192]{0:T(1024)S(1)}, bf16[8192,1,128]{2,0,1:T(8,128)(2,1)}, bf16[8192,1,128]{2,0,1:...) while((s32[]{:T(128)}, ...), condition=%wide.region_7.8_spmd, body=%wide.region_2.7_spmd.sunk | while | flops 139200528 | bytes 5046980 | solution.py:66
  198.7 6.3 %while.41 = (s32[]{:T(128)}, f32[1,512]{1,0:T(1,128)S(1)}, f32[1,512]{1,0:T(1,128)S(1)}, f32[1,512,128]{2,1,0:T(8,128)S(1)}, s32[]{:T(128)}, /*index=5*/s32[512]...) while((s32[]{:T(128)}, f32[1,512]{1,0:T(1,128)S(1)}, ...), condition=%wide.region_6.6_spmd.clone, body=%wide.region_3.5_spmd.clone.sunk | while | flops 139069440 | bytes 4118723 | solution.py:54
  209.2 9.5 %while.41 = (s32[]{:T(128)}, f32[1,512]{1,0:T(1,128)S(1)}, f32[1,512]{1,0:T(1,128)S(1)}, f32[1,512,128]{2,1,0:T(8,128)S(1)}, s32[]{:T(128)}, /*index=5*/s32[512]...) while((s32[]{:T(128)}, f32[1,512]{1,0:T(1,128)S(1)}, ...), condition=%wide.region_6.6_spmd.clone, body=%wide.region_3.5_spmd.clone.sunk | while | flops 139069440 | bytes 4118723 | solution.py:54
  222.9 12.6 %while.41 = (s32[]{:T(128)}, f32[1,512]{1,0:T(1,128)S(1)}, f32[1,512]{1,0:T(1,128)S(1)}, f32[1,512,128]{2,1,0:T(8,128)S(1)}, s32[]{:T(128)}, /*index=5*/s32[512]...) while((s32[]{:T(128)}, f32[1,512]{1,0:T(1,128)S(1)}, ...), condition=%wide.region_6.6_spmd.clone, body=%wide.region_3.5_spmd.clone.sunk | while | flops 139069440 | bytes 4118723 | solution.py:54
  239.8 6.3 %while.41 = (s32[]{:T(128)}, f32[1,512]{1,0:T(1,128)S(1)}, f32[1,512]{1,0:T(1,128)S(1)}, f32[1,512,128]{2,1,0:T(8,128)S(1)}, s32[]{:T(128)}, /*index=5*/s32[512]...) while((s32[]{:T(128)}, f32[1,512]{1,0:T(1,128)S(1)}, ...), condition=%wide.region_6.6_spmd.clone, body=%wide.region_3.5_spmd.clone.sunk | while | flops 139069440 | bytes 4118723 | solution.py:54
  250.4 6.3 %while.41 = (s32[]{:T(128)}, f32[1,512]{1,0:T(1,128)S(1)}, f32[1,512]{1,0:T(1,128)S(1)}, f32[1,512,128]{2,1,0:T(8,128)S(1)}, s32[]{:T(128)}, /*index=5*/s32[512]...) while((s32[]{:T(128)}, f32[1,512]{1,0:T(1,128)S(1)}, ...), condition=%wide.region_6.6_spmd.clone, body=%wide.region_3.5_spmd.clone.sunk | while | flops 139069440 | bytes 4118723 | solution.py:54
  260.9 9.5 %while.41 = (s32[]{:T(128)}, f32[1,512]{1,0:T(1,128)S(1)}, f32[1,512]{1,0:T(1,128)S(1)}, f32[1,512,128]{2,1,0:T(8,128)S(1)}, s32[]{:T(128)}, /*index=5*/s32[512]...) while((s32[]{:T(128)}, f32[1,512]{1,0:T(1,128)S(1)}, ...), condition=%wide.region_6.6_spmd.clone, body=%wide.region_3.5_spmd.clone.sunk | while | flops 139069440 | bytes 4118723 | solution.py:54
  274.6 12.6 %while.41 = (s32[]{:T(128)}, f32[1,512]{1,0:T(1,128)S(1)}, f32[1,512]{1,0:T(1,128)S(1)}, f32[1,512,128]{2,1,0:T(8,128)S(1)}, s32[]{:T(128)}, /*index=5*/s32[512]...) while((s32[]{:T(128)}, f32[1,512]{1,0:T(1,128)S(1)}, ...), condition=%wide.region_6.6_spmd.clone, body=%wide.region_3.5_spmd.clone.sunk | while | flops 139069440 | bytes 4118723 | solution.py:54
  291.5 15.8 %while.41 = (s32[]{:T(128)}, f32[1,512]{1,0:T(1,128)S(1)}, f32[1,512]{1,0:T(1,128)S(1)}, f32[1,512,128]{2,1,0:T(8,128)S(1)}, s32[]{:T(128)}, /*index=5*/s32[512]...) while((s32[]{:T(128)}, f32[1,512]{1,0:T(1,128)S(1)}, ...), condition=%wide.region_6.6_spmd.clone, body=%wide.region_3.5_spmd.clone.sunk | while | flops 139069440 | bytes 4118723 | solution.py:54
  311.5 18.9 %while.41 = (s32[]{:T(128)}, f32[1,512]{1,0:T(1,128)S(1)}, f32[1,512]{1,0:T(1,128)S(1)}, f32[1,512,128]{2,1,0:T(8,128)S(1)}, s32[]{:T(128)}, /*index=5*/s32[512]...) while((s32[]{:T(128)}, f32[1,512]{1,0:T(1,128)S(1)}, ...), condition=%wide.region_6.6_spmd.clone, body=%wide.region_3.5_spmd.clone.sunk | while | flops 139069440 | bytes 4118723 | solution.py:54
  334.7 22.1 %while.41 = (s32[]{:T(128)}, f32[1,512]{1,0:T(1,128)S(1)}, f32[1,512]{1,0:T(1,128)S(1)}, f32[1,512,128]{2,1,0:T(8,128)S(1)}, s32[]{:T(128)}, /*index=5*/s32[512]...) while((s32[]{:T(128)}, f32[1,512]{1,0:T(1,128)S(1)}, ...), condition=%wide.region_6.6_spmd.clone, body=%wide.region_3.5_spmd.clone.sunk | while | flops 139069440 | bytes 4118723 | solution.py:54
  361.0 25.2 %while.41 = (s32[]{:T(128)}, f32[1,512]{1,0:T(1,128)S(1)}, f32[1,512]{1,0:T(1,128)S(1)}, f32[1,512,128]{2,1,0:T(8,128)S(1)}, s32[]{:T(128)}, /*index=5*/s32[512]...) while((s32[]{:T(128)}, f32[1,512]{1,0:T(1,128)S(1)}, ...), condition=%wide.region_6.6_spmd.clone, body=%wide.region_3.5_spmd.clone.sunk | while | flops 139069440 | bytes 4118723 | solution.py:54
  390.4 28.4 %while.41 = (s32[]{:T(128)}, f32[1,512]{1,0:T(1,128)S(1)}, f32[1,512]{1,0:T(1,128)S(1)}, f32[1,512,128]{2,1,0:T(8,128)S(1)}, s32[]{:T(128)}, /*index=5*/s32[512]...) while((s32[]{:T(128)}, f32[1,512]{1,0:T(1,128)S(1)}, ...), condition=%wide.region_6.6_spmd.clone, body=%wide.region_3.5_spmd.clone.sunk | while | flops 139069440 | bytes 4118723 | solution.py:54
  423.1 6.3 %while.41 = (s32[]{:T(128)}, f32[1,512]{1,0:T(1,128)S(1)}, f32[1,512]{1,0:T(1,128)S(1)}, f32[1,512,128]{2,1,0:T(8,128)S(1)}, s32[]{:T(128)}, /*index=5*/s32[512]...) while((s32[]{:T(128)}, f32[1,512]{1,0:T(1,128)S(1)}, ...), condition=%wide.region_6.6_spmd.clone, body=%wide.region_3.5_spmd.clone.sunk | while | flops 139069440 | bytes 4118723 | solution.py:54
  433.6 9.5 %while.41 = (s32[]{:T(128)}, f32[1,512]{1,0:T(1,128)S(1)}, f32[1,512]{1,0:T(1,128)S(1)}, f32[1,512,128]{2,1,0:T(8,128)S(1)}, s32[]{:T(128)}, /*index=5*/s32[512]...) while((s32[]{:T(128)}, f32[1,512]{1,0:T(1,128)S(1)}, ...), condition=%wide.region_6.6_spmd.clone, body=%wide.region_3.5_spmd.clone.sunk | while | flops 139069440 | bytes 4118723 | solution.py:54
  447.3 6.3 %while.41 = (s32[]{:T(128)}, f32[1,512]{1,0:T(1,128)S(1)}, f32[1,512]{1,0:T(1,128)S(1)}, f32[1,512,128]{2,1,0:T(8,128)S(1)}, s32[]{:T(128)}, /*index=5*/s32[512]...) while((s32[]{:T(128)}, f32[1,512]{1,0:T(1,128)S(1)}, ...), condition=%wide.region_6.6_spmd.clone, body=%wide.region_3.5_spmd.clone.sunk | while | flops 139069440 | bytes 4118723 | solution.py:54
  461.3 56.7 %all_to_all.69 = bf16[64,2,8192]{2,1,0:T(2,128)(2,1)S(1)} all-to-all(bf16[64,2,8192]{2,1,0:T(2,128)(2,1)} %reshape.93), channel_id=1, replica_groups=mesh['rep'=8,'head'=64] {'head'}, dimensions={0} | all-to-all | bytes 4194304 | tf_op jit(solution)/shard_map/all_to_all | solution.py:87
  518.0 6.8 %reshape.94 = bf16[8192,1,128]{2,1,0:T(2,128)(2,1)} reshape(bf16[64,2,8192]{2,1,0:T(2,128)(2,1)S(1)} %all_to_all.69) | data formatting | bytes 4194304
  (577 shorter events, 254.2 us)
Async XLA Ops:
  4.1 14.0 %copy-start = (bf16[1,128,1024]{2,1,0:T(8,128)(2,1)S(1)}, bf16[1,128,1024]{2,1,0:T(8,128)(2,1)}, u32[]{:S(2)}) copy-start(bf16[1,128,1024]{2,1,0:T(8,128)(2,1)} %param.9) | copy-start | bytes 786436
  4.1 65.2 %all-to-all-start = ((bf16[128,64,128]{0,2,1:T(8,128)(2,1)}), bf16[128,64,128]{0,2,1:T(8,128)(2,1)S(1)}, u32[]{:S(2)}, u32[]{:S(2)}) async-start(bf16[128,64,128]{0,2,1:T(8,128)(2,1)} %bitcast.87), calls=%async_computation | async-start | bytes 4194304 | tf_op jit(solution)/shard_map/all_to_all | solution.py:80
  71.2 5.7 %copy-start.1 = (bf16[1,128,1024]{2,1,0:T(8,128)(2,1)S(1)}, bf16[1,128,1024]{2,1,0:T(8,128)(2,1)}, u32[]{:S(2)}) copy-start(bf16[1,128,1024]{2,1,0:T(8,128)(2,1)} %param.10) | copy-start | bytes 786436
  71.2 56.9 %all-to-all-start.1 = ((bf16[128,64,128]{2,0,1:T(8,128)(2,1)}), bf16[128,64,128]{2,0,1:T(8,128)(2,1)}, u32[]{:S(2)}, u32[]{:S(2)}) async-start(bf16[128,64,128]{2,0,1:T(8,128)(2,1)} %bitcast.86), calls=%async_computation.1 | async-start | bytes 4194304 | tf_op jit(solution)/shard_map/all_to_all | solution.py:81
  130.0 5.7 %copy-start.2 = (s32[1,8]{1,0:T(1,128)S(1)}, s32[1,8]{1,0:T(1,128)}, u32[]{:S(2)}) copy-start(s32[1,8]{1,0:T(1,128)} %param.11) | copy-start | bytes 100
  130.0 56.9 %all-to-all-start.2 = ((bf16[128,64,128]{2,0,1:T(8,128)(2,1)}), bf16[128,64,128]{2,0,1:T(8,128)(2,1)}, u32[]{:S(2)}, u32[]{:S(2)}) async-start(bf16[128,64,128]{2,0,1:T(8,128)(2,1)} %bitcast.85), calls=%async_computation.2 | async-start | bytes 4194304 | tf_op jit(solution)/shard_map/all_to_all | solution.py:82
where the time goes:
time: 538 us; the launch traced here: 534 us
  matrix products  173 us (32%)
  waiting for transfers between devices  150 us (28%)
  local copies, waits for them, and re-layouts  57.1 us (11%)
  blocking collectives  56.7 us (11%)
  loops' own time  44 us (8%)
  other arithmetic  27.8 us (5%)
  starting transfers between devices  25.4 us (5%)
    dot_general x63, matrix products, visit(): jnp.einsum('hqk,khd->hqd', weights.astype(jnp.bfloat16), v_block, preferr...  91.3 us
    dot_general x63, matrix products, visit(): jnp.einsum('qhd,khd->hqk', q_block, k_block, preferred_element_type=jnp.f...  81.5 us
    all_to_all x1, blocking collectives, local(): lax.all_to_all(outputs, 'head', split_axis=0, concat_axis=1, tiled=True)  56.7 us
    all_to_all x1, waiting for transfers between devices, local(): lax.all_to_all(q_heads, 'head', split_axis=1, concat_axis=0, tiled=True)  51.2 us
    all_to_all x1, waiting for transfers between devices, local(): lax.all_to_all(k_heads, 'head', split_axis=1, concat_axis=0, tiled=True)  51.1 us
    all_to_all x1, waiting for transfers between devices, local(): lax.all_to_all(v_heads, 'head', split_axis=1, concat_axis=0, tiled=True)  48 us
    another operation x1, loops' own time, attend_range(): return lax.fori_loop(lower, upper, place, blank)  40.2 us
    reduce_sum x63, other arithmetic, visit(): total = total * factor + jnp.sum(weights, axis=2)  20 us
  transfers between devices with their start and end apart: 3, of which 3 were waited for; matrix products, arithmetic and copies ran while one was open for 1% of the time, Pallas kernels for 0%

commit v1 on v0

v1 whole, which is shorter than its diff:
```python
import functools

import jax
import jax.numpy as jnp
from jax import lax
from jax.experimental import pallas as pl
from jax.experimental.pallas import tpu as pltpu
from jax.sharding import PartitionSpec as P

MESH = pl.DeviceIdType.MESH
F32 = jnp.float32
BF16 = jnp.bfloat16

HEADS = 8
DIM = 128
DOCS = 8
GROUP = 8
TOK = 128
SLICE = GROUP * TOK
WINDOW = 4
QB = 512
LOG2E_SCALE = 1.4426950408889634 * DIM**-0.5
OFF = -1e30


def kernel(slices, lengths, q_in, k_in, v_in, out, qb, kb, vt, v_raw, v_turned, q_doc, k_doc,
           top, total, accum, held, held_top, done,
           q_send, q_recv, kv_send, kv_recv, ring_send, ring_recv, out_send, out_recv, local_sem):
    rep = lax.axis_index("rep")
    me = lax.axis_index("head")
    z, g = me // GROUP, me % GROUP

    def peer(t):
        return (g + t) % GROUP

    def source(t):
        return (g - t + GROUP) % GROUP

    def device(zz, gg):
        return (rep, zz * GROUP + gg)

    def block(i, size=TOK):
        return pl.ds(pl.multiple_of(i * size, size), size)

    barrier = pltpu.get_barrier_semaphore()
    for t in range(1, GROUP):
        pl.semaphore_signal(barrier, inc=1, device_id=device(z, peer(t)), device_id_type=MESH)
    for step in (1, slices - 1):
        pl.semaphore_signal(barrier, inc=1, device_id=device((z + step) % slices, g), device_id_type=MESH)
    v_load = pltpu.make_async_copy(v_in, v_raw, local_sem.at[0])
    v_load.start()
    pl.semaphore_wait(barrier, GROUP + 1)

    def k_copy(t, to, row):
        src, dst = k_in.at[:, block(to)], kb.at[0, block(row), :]
        if t == 0:
            return pltpu.make_async_copy(src, dst, local_sem.at[1])
        return pltpu.make_async_remote_copy(src, dst, kv_send.at[0, t], kv_recv.at[0, t], device_id=device(z, to), device_id_type=MESH)

    def v_copy(t, to, row):
        src, dst = v_turned.at[to], vt.at[0, :, block(row)]
        if t == 0:
            return pltpu.make_async_copy(src, dst, local_sem.at[2])
        return pltpu.make_async_remote_copy(src, dst, kv_send.at[1, t], kv_recv.at[1, t], device_id=device(z, to), device_id_type=MESH)

    def q_copy(h, t, to, row):
        src, dst = q_in.at[:, block(to * HEADS + h)], qb.at[h, block(row), :]
        if t == 0:
            return pltpu.make_async_copy(src, dst, q_recv.at[h, 0])
        return pltpu.make_async_remote_copy(src, dst, q_send.at[h, t], q_recv.at[h, t], device_id=device(z, to), device_id_type=MESH)

    def out_copy(h, t, to, head_group):
        src, dst = done.at[h, block(to), :], out.at[:, block(head_group * HEADS + h)]
        if t == 0:
            return pltpu.make_async_copy(src, dst, out_recv.at[h, 0])
        return pltpu.make_async_remote_copy(src, dst, out_send.at[h, t], out_recv.at[h, t], device_id=device(z, to), device_id_type=MESH)

    def ring_copies(s):
        to = device((z + 1) % slices, g)
        return [
            pltpu.make_async_remote_copy(kb.at[s], kb.at[s + 1], ring_send.at[s, 0], ring_recv.at[s, 0], device_id=to, device_id_type=MESH),
            pltpu.make_async_remote_copy(vt.at[s], vt.at[s + 1], ring_send.at[s, 1], ring_recv.at[s, 1], device_id=to, device_id_type=MESH),
        ]

    for t in range(GROUP):
        k_copy(t, peer(t), g).start()
    v_load.wait()
    for i in range(GROUP):
        v_turned[i] = v_raw[:, i * TOK:(i + 1) * TOK].astype(F32).T.astype(BF16)
    for t in range(GROUP):
        v_copy(t, peer(t), g).start()

    def send_queries(h, _):
        for t in range(GROUP):
            q_copy(h, t, peer(t), g).start()
        return 0

    lax.fori_loop(0, HEADS, send_queries, 0)

    lane = lax.broadcasted_iota(jnp.int32, (1, DIM), 1)
    first = jnp.zeros((1, DIM), jnp.int32)
    last = jnp.zeros((1, DIM), jnp.int32)
    end = jnp.int32(0)
    for d in range(DOCS):
        begin = end
        end = end + lengths[0, d]
        first = jnp.where(lane == d, begin, first)
        last = jnp.where(lane == d, end, last)
    row = lax.broadcasted_iota(jnp.int32, (SLICE, DIM), 0)

    def within(base):
        spot = row + base
        return (spot >= first) & (spot < last)

    q_doc[...] = jnp.where(within(z * SLICE) | (lane >= DOCS), jnp.float32(0), jnp.float32(OFF)).astype(BF16)

    def fill(s, _):
        k_doc[s] = jnp.where(within((z - s) * SLICE), jnp.float32(1), jnp.float32(0)).astype(BF16)
        return 0

    lax.fori_loop(0, WINDOW + 1, fill, 0)

    def scores(h, step):
        b, s, lo, hi, diagonal = step
        query = jnp.concatenate([qb[h, b * QB:(b + 1) * QB, :], q_doc[b * QB:(b + 1) * QB, :]], axis=1)
        keys = jnp.concatenate([kb[s, lo:hi, :], k_doc[s, lo:hi, :]], axis=1)
        found = lax.dot_general(keys, query, (((1,), (1,)), ((), ())), preferred_element_type=F32)
        if diagonal:
            k_pos = lax.broadcasted_iota(jnp.int32, found.shape, 0) + lo
            q_pos = lax.broadcasted_iota(jnp.int32, found.shape, 1) + b * QB
            found = jnp.where(k_pos <= q_pos, found, jnp.float32(OFF))
        return found, jnp.max(found, axis=0, keepdims=True)

    def unit(h, steps, fresh=False, following=None):
        state = {}
        now = (held[...], held_top[...]) if following is not None else scores(h, steps[0])
        for i, (b, s, lo, hi, _) in enumerate(steps):
            cols = slice(b * QB, (b + 1) * QB)
            later = None
            if i + 1 < len(steps):
                later = scores(h, steps[i + 1])
            elif following is not None:
                held[...], held_top[...] = scores(following, steps[0])
            found, best = now
            if b not in state and not fresh:
                state[b] = (top[h, :, cols], total[h, :, cols], accum[h, :, cols])
            if b in state:
                old, norm, acc = state[b]
                best = jnp.maximum(old, best)
            weights = jnp.exp2((found - best) * LOG2E_SCALE)
            product = jnp.dot(vt[s, :, lo:hi], weights.astype(BF16), preferred_element_type=F32)
            added = jnp.sum(weights, axis=0, keepdims=True)
            if b in state:
                factor = jnp.exp2((old - best) * LOG2E_SCALE)
                state[b] = (best, norm * factor + added, acc * factor + product)
            else:
                state[b] = (best, added, product)
            if not any(other[0] == b for other in steps[i + 1:]):
                top[h, :, cols], total[h, :, cols], accum[h, :, cols] = state[b]
            now = later

    blocks = SLICE // QB
    diag = [(b, 0, 0, (b + 1) * QB, True) for b in range(blocks)]
    far = [(b, WINDOW, b * QB, SLICE, False) for b in range(blocks)]

    def full(s):
        return [(b, s, 0, SLICE, False) for b in range(blocks)]

    def sweep(lo, hi, steps, before=None, after=None):
        held[...], held_top[...] = scores(lo, steps[0])

        def body(h, _):
            if before is not None:
                before(h)
            unit(h, steps, following=jnp.minimum(h + 1, hi - 1))
            if after is not None:
                after(h)
            return 0

        lax.fori_loop(lo, hi, body, 0)

    def wait_queries(h):
        for t in range(GROUP):
            copy = q_copy(h, t, g, source(t))
            copy.wait() if t == 0 else copy.wait_recv()

    def arrive(s):
        @pl.when(z >= s)
        def _():
            for copy in ring_copies(s - 1):
                copy.wait_recv()

    def pass_on(s):
        @pl.when((z >= s) & (z < slices - 1))
        def _():
            for copy in ring_copies(s):
                copy.start()

    def finish(h):
        for b in range(blocks):
            cols = slice(b * QB, (b + 1) * QB)
            done[h, cols, :] = (accum[h, :, cols] / total[h, :, cols]).T.astype(BF16)
        for t in range(GROUP):
            out_copy(h, t, peer(t), g).start()

    for t in range(GROUP):
        copy = k_copy(t, g, source(t))
        copy.wait() if t == 0 else copy.wait_recv()
    for t in range(GROUP):
        copy = v_copy(t, g, source(t))
        copy.wait() if t == 0 else copy.wait_recv()
    pass_on(0)

    half = HEADS // 2

    def opening(h, _):
        wait_queries(h)
        unit(h, diag, fresh=True)
        return 0

    lax.fori_loop(0, half, opening, 0)
    arrive(1)
    pass_on(1)

    @pl.when(z >= 1)
    def _():
        sweep(0, half, full(1))

    def middle(h, _):
        wait_queries(h)

        @pl.when(h == half + 2)
        def _():
            arrive(2)
            pass_on(2)

        @pl.when(z >= 1)
        def _():
            unit(h, diag + full(1), fresh=True)

        @pl.when(z < 1)
        def _():
            unit(h, diag, fresh=True)

        return 0

    lax.fori_loop(half, HEADS, middle, 0)

    def relay(h):
        @pl.when(h == half)
        def _():
            arrive(3)
            pass_on(3)

    @pl.when(z >= 2)
    def _():
        sweep(0, HEADS, full(2), before=relay)

    def last_wait(h):
        @pl.when(h == 0)
        def _():
            arrive(4)

    @pl.when(z >= 4)
    def _():
        sweep(0, HEADS, full(3) + far, before=last_wait, after=finish)

    @pl.when(z == 3)
    def _():
        sweep(0, HEADS, full(3), after=finish)

    @pl.when(z < 3)
    def _():
        def body(h, _):
            finish(h)
            return 0

        lax.fori_loop(0, HEADS, body, 0)

    for t in range(1, GROUP):
        k_copy(t, peer(t), g).wait_send()
        v_copy(t, peer(t), g).wait_send()
    for s in range(WINDOW):
        @pl.when((z >= s) & (z < slices - 1))
        def _():
            for copy in ring_copies(s):
                copy.wait_send()

    def closing(h, _):
        for t in range(1, GROUP):
            q_copy(h, t, peer(t), g).wait_send()
            out_copy(h, t, peer(t), g).wait_send()
        for t in range(GROUP):
            copy = out_copy(h, t, g, source(t))
            copy.wait() if t == 0 else copy.wait_recv()
        return 0

    lax.fori_loop(0, HEADS, closing, 0)


def solution(mesh):
    slices = mesh.shape["head"] // GROUP

    def local(query, key, value, lengths):
        rows, width = query.shape[1:]
        hbm = pl.BlockSpec(memory_space=pl.ANY)
        dma = pltpu.SemaphoreType.DMA
        attended = pl.pallas_call(
            functools.partial(kernel, slices),
            out_shape=jax.ShapeDtypeStruct((rows, width), BF16),
            in_specs=[pl.BlockSpec(memory_space=pltpu.SMEM), hbm, hbm, hbm],
            out_specs=hbm,
            scratch_shapes=[
                pltpu.VMEM((HEADS, SLICE, DIM), BF16),
                pltpu.VMEM((WINDOW + 1, SLICE, DIM), BF16),
                pltpu.VMEM((WINDOW + 1, DIM, SLICE), BF16),
                pltpu.VMEM((TOK, GROUP * DIM), BF16),
                pltpu.VMEM((GROUP, DIM, TOK), BF16),
                pltpu.VMEM((SLICE, DIM), BF16),
                pltpu.VMEM((WINDOW + 1, SLICE, DIM), BF16),
                pltpu.VMEM((HEADS, 1, SLICE), F32),
                pltpu.VMEM((HEADS, 1, SLICE), F32),
                pltpu.VMEM((HEADS, DIM, SLICE), F32),
                pltpu.VMEM((SLICE, QB), F32),
                pltpu.VMEM((1, QB), F32),
                pltpu.VMEM((HEADS, SLICE, DIM), BF16),
                dma((HEADS, GROUP)),
                dma((HEADS, GROUP)),
                dma((2, GROUP)),
                dma((2, GROUP)),
                dma((WINDOW, 2)),
                dma((WINDOW, 2)),
                dma((HEADS, GROUP)),
                dma((HEADS, GROUP)),
                dma((3,)),
            ],
            compiler_params=pltpu.CompilerParams(collective_id=0, has_side_effects=True, vmem_limit_bytes=56 * 2**20),
        )(lengths, query[0], key[0], value[0])
        return attended[None]

    placed = (P("rep", "head", None), P("rep", "head", None), P("rep", "head", None), P("rep", None))
    return jax.shard_map(local, mesh=mesh, in_specs=placed, out_specs=P("rep", "head", None), check_vma=False)
```

time: 538 us -> 99.4 us (0.18)
  the two profiles are of different devices: /device:TPU:54 before, /device:TPU:289 now
where the time goes in v1:
time: 99.4 us; the launch traced here: 99.2 us
  Pallas kernels  96.1 us (97%)
  local copies, waits for them, and re-layouts  3.1 us (3%)
    pallas_call x1, Pallas kernels, local(): pl.pallas_call(functools.partial(kernel, slices), out_shape=jax.ShapeDtyp...  96.1 us
    unnamed x1, local copies, waits for them, and re-layouts  3.1 us

profile of v1, /device:TPU:289, one launch (start us, length us, event | category | flops | bytes accessed | tf_op | source)
XLA Modules:
  0.0 99.2 jit_solution(14727085290497622720)
XLA Ops:
  0.0 96.1 %shard_map.46 = bf16[128,8192]{1,0:T(8,128)(2,1)} custom-call(s32[1,8]{1,0:T(1,128)} %lengths.1, bf16[128,8192]{1,0:T(8,128)(2,1)} %bitcast.5, bf16[128,1024]{1,0:T(8,128)(2,1)} %bitcast.6, bf16[128,1024]{1,0:T(8,128)(2,1)} %bitcast.7), custom_call_target="tpu_custom_call" | custom-call | tf_op jit(solution)/shard_map/pallas_call | solution.py:308
  96.1 3.1 %copy.6 = bf16[1,128,8192]{2,1,0:T(8,128)(2,1)} copy(bf16[1,128,8192]{2,1,0:T(8,128)(2,1)} %bitcast.4) | data formatting | bytes 4194304

commit v2 on v1

--- a/solution.py
+++ b/solution.py
@@ -17,6 +17,7 @@
 GROUP = 8
 TOK = 128
 SLICE = GROUP * TOK
+HALF = SLICE // 2
 WINDOW = 4
 QB = 512
 LOG2E_SCALE = 1.4426950408889634 * DIM**-0.5
@@ -25,7 +26,8 @@
 
 def kernel(slices, lengths, q_in, k_in, v_in, out, qb, kb, vt, v_raw, v_turned, q_doc, k_doc,
            top, total, accum, held, held_top, done,
-           q_send, q_recv, kv_send, kv_recv, ring_send, ring_recv, out_send, out_recv, local_sem):
+           k_relay, v_relay,
+           q_send, q_recv, kv_send, kv_recv, ring_send, ring_recv, back_send, back_recv, out_send, out_recv, local_sem, ready):
     rep = lax.axis_index("rep")
     me = lax.axis_index("head")
     z, g = me // GROUP, me % GROUP
@@ -33,66 +35,89 @@
     def peer(t):
         return (g + t) % GROUP
 
-    def source(t):
-        return (g - t + GROUP) % GROUP
-
     def device(zz, gg):
         return (rep, zz * GROUP + gg)
 
     def block(i, size=TOK):
         return pl.ds(pl.multiple_of(i * size, size), size)
 
+    def when(condition, action):
+        pl.when(condition)(action)
+
     barrier = pltpu.get_barrier_semaphore()
+
+    def greet(zz):
+        pl.semaphore_signal(barrier, inc=1, device_id=device(zz, g), device_id_type=MESH)
+
+    def answer(i, zz):
+        pl.semaphore_signal(ready.at[i], inc=1, device_id=device(zz, g), device_id_type=MESH)
+
+    v_load = pltpu.make_async_copy(v_in, v_raw, local_sem.at[0])
+    v_load.start()
     for t in range(1, GROUP):
         pl.semaphore_signal(barrier, inc=1, device_id=device(z, peer(t)), device_id_type=MESH)
-    for step in (1, slices - 1):
-        pl.semaphore_signal(barrier, inc=1, device_id=device((z + step) % slices, g), device_id_type=MESH)
-    v_load = pltpu.make_async_copy(v_in, v_raw, local_sem.at[0])
-    v_load.start()
-    pl.semaphore_wait(barrier, GROUP + 1)
-
-    def k_copy(t, to, row):
-        src, dst = k_in.at[:, block(to)], kb.at[0, block(row), :]
+    when(z < slices - 1, lambda: greet(z + 1))
+    when(z == 0, lambda: greet(slices - 1))
+    when(z == WINDOW, lambda: greet(slices - 1))
+    when(z < slices - 1 - WINDOW, lambda: greet(z + 1 + WINDOW))
+    expected = jnp.where(z > 0, GROUP, GROUP - 1) + jnp.where(z > WINDOW, 1, 0) + jnp.where(z == slices - 1, 2, 0)
+    pl.semaphore_wait(barrier, expected)
+    when(z > 0, lambda: answer(0, z - 1))
+    when(z == slices - 1, lambda: answer(1, 0))
+    when(z > WINDOW, lambda: answer(2, z - 1 - WINDOW))
+
+    def copy_to(t, src, dst, send, recv):
         if t == 0:
-            return pltpu.make_async_copy(src, dst, local_sem.at[1])
-        return pltpu.make_async_remote_copy(src, dst, kv_send.at[0, t], kv_recv.at[0, t], device_id=device(z, to), device_id_type=MESH)
-
-    def v_copy(t, to, row):
-        src, dst = v_turned.at[to], vt.at[0, :, block(row)]
-        if t == 0:
-            return pltpu.make_async_copy(src, dst, local_sem.at[2])
-        return pltpu.make_async_remote_copy(src, dst, kv_send.at[1, t], kv_recv.at[1, t], device_id=device(z, to), device_id_type=MESH)
-
-    def q_copy(h, t, to, row):
-        src, dst = q_in.at[:, block(to * HEADS + h)], qb.at[h, block(row), :]
-        if t == 0:
-            return pltpu.make_async_copy(src, dst, q_recv.at[h, 0])
-        return pltpu.make_async_remote_copy(src, dst, q_send.at[h, t], q_recv.at[h, t], device_id=device(z, to), device_id_type=MESH)
-
-    def out_copy(h, t, to, head_group):
-        src, dst = done.at[h, block(to), :], out.at[:, block(head_group * HEADS + h)]
-        if t == 0:
-            return pltpu.make_async_copy(src, dst, out_recv.at[h, 0])
-        return pltpu.make_async_remote_copy(src, dst, out_send.at[h, t], out_recv.at[h, t], device_id=device(z, to), device_id_type=MESH)
-
-    def ring_copies(s):
-        to = device((z + 1) % slices, g)
-        return [
-            pltpu.make_async_remote_copy(kb.at[s], kb.at[s + 1], ring_send.at[s, 0], ring_recv.at[s, 0], device_id=to, device_id_type=MESH),
-            pltpu.make_async_remote_copy(vt.at[s], vt.at[s + 1], ring_send.at[s, 1], ring_recv.at[s, 1], device_id=to, device_id_type=MESH),
-        ]
+            return pltpu.make_async_copy(src, dst, recv)
+        return pltpu.make_async_remote_copy(src, dst, send, recv, device_id=device(z, peer(t)), device_id_type=MESH)
+
+    def k_copy(t):
+        return copy_to(t, k_in.at[:, block(peer(t))], kb.at[0, block(g), :], kv_send.at[0], kv_recv.at[0])
+
+    def v_copy(t):
+        return copy_to(t, v_turned.at[peer(t)], vt.at[0, :, block(g)], kv_send.at[1], kv_recv.at[1])
+
+    def q_copy(h, t):
+        return copy_to(t, q_in.at[:, block(peer(t) * HEADS + h)], qb.at[h, block(g), :], q_send.at[0], q_recv.at[h])
+
+    def out_copy(h, t):
+        return copy_to(t, done.at[h, block(peer(t)), :], out.at[:, block(g * HEADS + h)], out_send.at[0], out_recv.at[0])
+
+    def wait_bytes(ref, sem):
+        pltpu.make_async_copy(ref, ref, sem).wait()
+
+    def half_refs(s, j):
+        part = pl.ds(j * HALF, HALF)
+        return kb.at[s, part, :], vt.at[s, :, part]
+
+    def remote(pairs, send, recv, to):
+        return [pltpu.make_async_remote_copy(src, dst, send, recv, device_id=device(to, g), device_id_type=MESH) for src, dst in pairs]
+
+    def ring_copies(s, j):
+        return remote(zip(half_refs(s, j), half_refs(s + 1, j)), ring_send.at[s, j], ring_recv.at[s, j], (z + 1) % slices)
+
+    def back_copies(hop):
+        if hop == 0:
+            return remote(zip(half_refs(0, 0), (k_relay, v_relay)), back_send.at[0], back_recv.at[0], (z + slices - 1) % slices)
+        return remote(zip((k_relay, v_relay), half_refs(WINDOW, 0)), back_send.at[1], back_recv.at[1], (z + WINDOW + 1) % slices)
+
+    def wait_half(sem):
+        wait_bytes(kb.at[0], sem)
+
+    sends_back = z < slices - WINDOW
+    relays = (z < slices - 1 - WINDOW) | (z == slices - 1)
 
     for t in range(GROUP):
-        k_copy(t, peer(t), g).start()
+        k_copy(t).start()
     v_load.wait()
     for i in range(GROUP):
         v_turned[i] = v_raw[:, i * TOK:(i + 1) * TOK].astype(F32).T.astype(BF16)
     for t in range(GROUP):
-        v_copy(t, peer(t), g).start()
+        v_copy(t).start()
 
     def send_queries(h, _):
         for t in range(GROUP):
-            q_copy(h, t, peer(t), g).start()
+            q_copy(h, t).start()
         return 0
 
     lax.fori_loop(0, HEADS, send_queries, 0)
@@ -180,59 +205,75 @@
         lax.fori_loop(lo, hi, body, 0)
 
     def wait_queries(h):
-        for t in range(GROUP):
-            copy = q_copy(h, t, g, source(t))
-            copy.wait() if t == 0 else copy.wait_recv()
-
-    def arrive(s):
-        @pl.when(z >= s)
-        def _():
-            for copy in ring_copies(s - 1):
-                copy.wait_recv()
-
-    def pass_on(s):
-        @pl.when((z >= s) & (z < slices - 1))
-        def _():
-            for copy in ring_copies(s):
+        wait_bytes(qb.at[h], q_recv.at[h])
+
+    def start(copies):
+        def act():
+            for copy in copies:
                 copy.start()
+        return act
+
+    def arrive(s, j):
+        when(z >= s, lambda: wait_half(ring_recv.at[s - 1, j]))
+
+    def pass_on(s, j):
+        when((z >= s) & (z < slices - 1), start(ring_copies(s, j)))
+
+    def relay_back():
+        when(z < slices - 1 - WINDOW, lambda: pl.semaphore_wait(ready.at[2], 1))
+        when(relays, lambda: wait_half(back_recv.at[0]))
+        when(relays, start(back_copies(1)))
 
     def finish(h):
         for b in range(blocks):
             cols = slice(b * QB, (b + 1) * QB)
             done[h, cols, :] = (accum[h, :, cols] / total[h, :, cols]).T.astype(BF16)
         for t in range(GROUP):
-            out_copy(h, t, peer(t), g).start()
-
-    for t in range(GROUP):
-        copy = k_copy(t, g, source(t))
-        copy.wait() if t == 0 else copy.wait_recv()
-    for t in range(GROUP):
-        copy = v_copy(t, g, source(t))
-        copy.wait() if t == 0 else copy.wait_recv()
-    pass_on(0)
+            out_copy(h, t).start()
+
+    wait_bytes(kb.at[0], kv_recv.at[0])
+    wait_bytes(vt.at[0], kv_recv.at[1])
+    when(z < slices - 1, lambda: pl.semaphore_wait(ready.at[0], 1))
+    pass_on(0, 1)
+    when(z == 0, lambda: pl.semaphore_wait(ready.at[1], 1))
+    when(sends_back, start(back_copies(0)))
 
     half = HEADS // 2
 
     def opening(h, _):
+        @pl.when(h == 2)
+        def _():
+            arrive(1, 1)
+            pass_on(1, 1)
+
         wait_queries(h)
+
+        @pl.when(h == 0)
+        def _():
+            pass_on(0, 0)
+
         unit(h, diag, fresh=True)
         return 0
 
     lax.fori_loop(0, half, opening, 0)
-    arrive(1)
-    pass_on(1)
+    arrive(1, 0)
+    pass_on(1, 0)
+    relay_back()
 
     @pl.when(z >= 1)
     def _():
         sweep(0, half, full(1))
+
+    arrive(2, 1)
+    pass_on(2, 1)
 
     def middle(h, _):
         wait_queries(h)
 
         @pl.when(h == half + 2)
         def _():
-            arrive(2)
-            pass_on(2)
+            arrive(2, 0)
+            pass_on(2, 0)
 
         @pl.when(z >= 1)
         def _():
@@ -247,23 +288,22 @@
     lax.fori_loop(half, HEADS, middle, 0)
 
     def relay(h):
-        @pl.when(h == half)
-        def _():
-            arrive(3)
-            pass_on(3)
+        @pl.when(h == 1)
+        def _():
+            arrive(3, 1)
+            pass_on(3, 1)
 
     @pl.when(z >= 2)
     def _():
         sweep(0, HEADS, full(2), before=relay)
 
-    def last_wait(h):
-        @pl.when(h == 0)
-        def _():
-            arrive(4)
-
-    @pl.when(z >= 4)
-    def _():
-        sweep(0, HEADS, full(3) + far, before=last_wait, after=finish)
+    arrive(3, 0)
+
+    @pl.when(z >= WINDOW)
+    def _():
+        wait_half(ring_recv.at[WINDOW - 1, 1])
+        wait_half(back_recv.at[1])
+        sweep(0, HEADS, full(3) + far, after=finish)
 
     @pl.when(z == 3)
     def _():
@@ -277,25 +317,18 @@
 
         lax.fori_loop(0, HEADS, body, 0)
 
-    for t in range(1, GROUP):
-        k_copy(t, peer(t), g).wait_send()
-        v_copy(t, peer(t), g).wait_send()
+    others = GROUP - 1
+    wait_bytes(kb.at[0, pl.ds(0, others * TOK), :], kv_send.at[0])
+    wait_bytes(v_turned.at[pl.ds(0, others)], kv_send.at[1])
+    wait_bytes(qb.at[pl.ds(0, others)], q_send.at[0])
     for s in range(WINDOW):
-        @pl.when((z >= s) & (z < slices - 1))
-        def _():
-            for copy in ring_copies(s):
-                copy.wait_send()
-
-    def closing(h, _):
-        for t in range(1, GROUP):
-            q_copy(h, t, peer(t), g).wait_send()
-            out_copy(h, t, peer(t), g).wait_send()
-        for t in range(GROUP):
-            copy = out_copy(h, t, g, source(t))
-            copy.wait() if t == 0 else copy.wait_recv()
-        return 0
-
-    lax.fori_loop(0, HEADS, closing, 0)
+        for j in range(2):
+            if (s, j) != (WINDOW - 1, 0):
+                when((z >= s) & (z < slices - 1), lambda s=s, j=j: wait_half(ring_send.at[s, j]))
+    when(sends_back, lambda: wait_half(back_send.at[0]))
+    when(relays, lambda: wait_half(back_send.at[1]))
+    wait_bytes(done.at[pl.ds(0, others)], out_send.at[0])
+    wait_bytes(out, out_recv.at[0])
 
 
 def solution(mesh):
@@ -324,15 +357,20 @@
                 pltpu.VMEM((SLICE, QB), F32),
                 pltpu.VMEM((1, QB), F32),
                 pltpu.VMEM((HEADS, SLICE, DIM), BF16),
-                dma((HEADS, GROUP)),
-                dma((HEADS, GROUP)),
-                dma((2, GROUP)),
-                dma((2, GROUP)),
+                pltpu.VMEM((HALF, DIM), BF16),
+                pltpu.VMEM((DIM, HALF), BF16),
+                dma((1,)),
+                dma((HEADS,)),
+                dma((2,)),
+                dma((2,)),
                 dma((WINDOW, 2)),
                 dma((WINDOW, 2)),
-                dma((HEADS, GROUP)),
-                dma((HEADS, GROUP)),
-                dma((3,)),
+                dma((2,)),
+                dma((2,)),
+                dma((1,)),
+                dma((1,)),
+                dma((1,)),
+                pltpu.SemaphoreType.REGULAR((3,)),
             ],
             compiler_params=pltpu.CompilerParams(collective_id=0, has_side_effects=True, vmem_limit_bytes=56 * 2**20),
         )(lengths, query[0], key[0], value[0])

time: 99.4 us -> 86.4 us (0.87)
  the two profiles are of different devices: /device:TPU:289 before, /device:TPU:257 now
where the time goes in v2:
time: 86.4 us; the launch traced here: 86.2 us
  Pallas kernels  83.1 us (96%)
  local copies, waits for them, and re-layouts  3.1 us (4%)
    pallas_call x1, Pallas kernels, local(): pl.pallas_call(functools.partial(kernel, slices), out_shape=jax.ShapeDtyp...  83.1 us
    unnamed x1, local copies, waits for them, and re-layouts  3.1 us

profile of v2, /device:TPU:257, one launch (start us, length us, event | category | flops | bytes accessed | tf_op | source)
XLA Modules:
  0.0 86.2 jit_solution(7398662766632822025)
XLA Ops:
  0.0 83.1 %shard_map.46 = bf16[128,8192]{1,0:T(8,128)(2,1)} custom-call(s32[1,8]{1,0:T(1,128)} %lengths.1, bf16[128,8192]{1,0:T(8,128)(2,1)} %bitcast.5, bf16[128,1024]{1,0:T(8,128)(2,1)} %bitcast.6, bf16[128,1024]{1,0:T(8,128)(2,1)} %bitcast.7), custom_call_target="tpu_custom_call" | custom-call | tf_op jit(solution)/shard_map/pallas_call | solution.py:341
  83.1 3.1 %copy.6 = bf16[1,128,8192]{2,1,0:T(8,128)(2,1)} copy(bf16[1,128,8192]{2,1,0:T(8,128)(2,1)} %bitcast.4) | data formatting | bytes 4194304

commit v3 on v2

--- a/solution.py
+++ b/solution.py
@@ -18,8 +18,11 @@
 TOK = 128
 SLICE = GROUP * TOK
 HALF = SLICE // 2
+BACK = SLICE * 3 // 4
+MOST = 6
 WINDOW = 4
 QB = 512
+EDGE = 256
 LOG2E_SCALE = 1.4426950408889634 * DIM**-0.5
 OFF = -1e30
 
@@ -86,23 +89,27 @@
     def wait_bytes(ref, sem):
         pltpu.make_async_copy(ref, ref, sem).wait()
 
-    def half_refs(s, j):
-        part = pl.ds(j * HALF, HALF)
+    def part_refs(s, lo, hi):
+        part = pl.ds(lo, hi - lo)
         return kb.at[s, part, :], vt.at[s, :, part]
 
     def remote(pairs, send, recv, to):
         return [pltpu.make_async_remote_copy(src, dst, send, recv, device_id=device(to, g), device_id_type=MESH) for src, dst in pairs]
 
     def ring_copies(s, j):
-        return remote(zip(half_refs(s, j), half_refs(s + 1, j)), ring_send.at[s, j], ring_recv.at[s, j], (z + 1) % slices)
+        lo, hi = (BACK, SLICE) if s == WINDOW - 1 else (j * HALF, (j + 1) * HALF)
+        return remote(zip(part_refs(s, lo, hi), part_refs(s + 1, lo, hi)), ring_send.at[s, j], ring_recv.at[s, j], (z + 1) % slices)
 
     def back_copies(hop):
         if hop == 0:
-            return remote(zip(half_refs(0, 0), (k_relay, v_relay)), back_send.at[0], back_recv.at[0], (z + slices - 1) % slices)
-        return remote(zip((k_relay, v_relay), half_refs(WINDOW, 0)), back_send.at[1], back_recv.at[1], (z + WINDOW + 1) % slices)
-
-    def wait_half(sem):
-        wait_bytes(kb.at[0], sem)
+            return remote(zip(part_refs(0, 0, BACK), (k_relay, v_relay)), back_send.at[0], back_recv.at[0], (z + slices - 1) % slices)
+        return remote(zip((k_relay, v_relay), part_refs(WINDOW, 0, BACK)), back_send.at[1], back_recv.at[1], (z + WINDOW + 1) % slices)
+
+    def wait_ring(sem, s):
+        wait_bytes(kb.at[0, pl.ds(0, 2 * (SLICE - BACK)), :] if s == WINDOW - 1 else kb.at[0], sem)
+
+    def wait_back(sem):
+        wait_bytes(kb.at[pl.ds(0, 3), pl.ds(0, 2 * BACK // 3), :], sem)
 
     sends_back = z < slices - WINDOW
     relays = (z < slices - 1 - WINDOW) | (z == slices - 1)
@@ -146,53 +153,61 @@
     lax.fori_loop(0, WINDOW + 1, fill, 0)
 
     def scores(h, step):
-        b, s, lo, hi, diagonal = step
-        query = jnp.concatenate([qb[h, b * QB:(b + 1) * QB, :], q_doc[b * QB:(b + 1) * QB, :]], axis=1)
+        q_lo, q_hi, s, lo, hi, diagonal = step
+        query = jnp.concatenate([qb[h, q_lo:q_hi, :], q_doc[q_lo:q_hi, :]], axis=1)
         keys = jnp.concatenate([kb[s, lo:hi, :], k_doc[s, lo:hi, :]], axis=1)
         found = lax.dot_general(keys, query, (((1,), (1,)), ((), ())), preferred_element_type=F32)
         if diagonal:
             k_pos = lax.broadcasted_iota(jnp.int32, found.shape, 0) + lo
-            q_pos = lax.broadcasted_iota(jnp.int32, found.shape, 1) + b * QB
+            q_pos = lax.broadcasted_iota(jnp.int32, found.shape, 1) + q_lo
             found = jnp.where(k_pos <= q_pos, found, jnp.float32(OFF))
         return found, jnp.max(found, axis=0, keepdims=True)
 
     def unit(h, steps, fresh=False, following=None):
         state = {}
-        now = (held[...], held_top[...]) if following is not None else scores(h, steps[0])
-        for i, (b, s, lo, hi, _) in enumerate(steps):
-            cols = slice(b * QB, (b + 1) * QB)
+        size = steps[0][4] - steps[0][3]
+        now = (held[:size, :], held_top[...]) if following is not None else scores(h, steps[0])
+        for i, (q_lo, q_hi, s, lo, hi, _) in enumerate(steps):
+            edges = range(q_lo, q_hi, EDGE)
             later = None
             if i + 1 < len(steps):
                 later = scores(h, steps[i + 1])
             elif following is not None:
-                held[...], held_top[...] = scores(following, steps[0])
+                held[:size, :], held_top[...] = scores(following, steps[0])
             found, best = now
-            if b not in state and not fresh:
-                state[b] = (top[h, :, cols], total[h, :, cols], accum[h, :, cols])
-            if b in state:
-                old, norm, acc = state[b]
+            for e in edges:
+                if e not in state and not fresh:
+                    cols = slice(e, e + EDGE)
+                    state[e] = (top[h, :, cols], total[h, :, cols], accum[h, :, cols])
+            known = edges[0] in state
+            if known:
+                old, norm, acc = (jnp.concatenate(parts, axis=1) for parts in zip(*(state[e] for e in edges)))
                 best = jnp.maximum(old, best)
             weights = jnp.exp2((found - best) * LOG2E_SCALE)
             product = jnp.dot(vt[s, :, lo:hi], weights.astype(BF16), preferred_element_type=F32)
             added = jnp.sum(weights, axis=0, keepdims=True)
-            if b in state:
+            if known:
                 factor = jnp.exp2((old - best) * LOG2E_SCALE)
-                state[b] = (best, norm * factor + added, acc * factor + product)
-            else:
-                state[b] = (best, added, product)
-            if not any(other[0] == b for other in steps[i + 1:]):
-                top[h, :, cols], total[h, :, cols], accum[h, :, cols] = state[b]
+                added, product = norm * factor + added, acc * factor + product
+            for e in edges:
+                part = slice(e - q_lo, e - q_lo + EDGE)
+                state[e] = (best[:, part], added[:, part], product[:, part])
+                if not any(other[0] <= e < other[1] for other in steps[i + 1:]):
+                    cols = slice(e, e + EDGE)
+                    top[h, :, cols], total[h, :, cols], accum[h, :, cols] = state[e]
             now = later
 
     blocks = SLICE // QB
-    diag = [(b, 0, 0, (b + 1) * QB, True) for b in range(blocks)]
-    far = [(b, WINDOW, b * QB, SLICE, False) for b in range(blocks)]
+    diag, far = [], []
+    for lo in range(0, SLICE, QB):
+        diag += [(lo, lo + QB, 0, 0, lo + EDGE, True), (lo + EDGE, lo + QB, 0, lo + EDGE, lo + QB, True)]
+        far += [(lo, lo + QB, WINDOW, lo + EDGE, SLICE, False), (lo, lo + EDGE, WINDOW, lo, lo + EDGE, False)]
 
     def full(s):
-        return [(b, s, 0, SLICE, False) for b in range(blocks)]
+        return [(lo, lo + QB, s, 0, SLICE, False) for lo in range(0, SLICE, QB)]
 
     def sweep(lo, hi, steps, before=None, after=None):
-        held[...], held_top[...] = scores(lo, steps[0])
+        held[:steps[0][4] - steps[0][3], :], held_top[...] = scores(lo, steps[0])
 
         def body(h, _):
             if before is not None:
@@ -214,14 +229,14 @@
         return act
 
     def arrive(s, j):
-        when(z >= s, lambda: wait_half(ring_recv.at[s - 1, j]))
+        when(z >= s, lambda: wait_ring(ring_recv.at[s - 1, j], s - 1))
 
     def pass_on(s, j):
         when((z >= s) & (z < slices - 1), start(ring_copies(s, j)))
 
     def relay_back():
         when(z < slices - 1 - WINDOW, lambda: pl.semaphore_wait(ready.at[2], 1))
-        when(relays, lambda: wait_half(back_recv.at[0]))
+        when(relays, lambda: wait_back(back_recv.at[0]))
         when(relays, start(back_copies(1)))
 
     def finish(h):
@@ -246,6 +261,7 @@
             arrive(1, 1)
             pass_on(1, 1)
 
+        when(h == half - 1, relay_back)
         wait_queries(h)
 
         @pl.when(h == 0)
@@ -258,7 +274,6 @@
     lax.fori_loop(0, half, opening, 0)
     arrive(1, 0)
     pass_on(1, 0)
-    relay_back()
 
     @pl.when(z >= 1)
     def _():
@@ -293,24 +308,25 @@
             arrive(3, 1)
             pass_on(3, 1)
 
-    @pl.when(z >= 2)
-    def _():
-        sweep(0, HEADS, full(2), before=relay)
-
+    when(z >= 2, lambda: sweep(0, MOST, full(2), before=relay))
     arrive(3, 0)
 
     @pl.when(z >= WINDOW)
     def _():
-        wait_half(ring_recv.at[WINDOW - 1, 1])
-        wait_half(back_recv.at[1])
-        sweep(0, HEADS, full(3) + far, after=finish)
+        wait_back(back_recv.at[1])
+        wait_ring(ring_recv.at[WINDOW - 1, 1], WINDOW - 1)
+        sweep(0, MOST, full(3) + far, after=finish)
+        sweep(MOST, HEADS, full(2) + full(3) + far, after=finish)
 
     @pl.when(z == 3)
     def _():
-        sweep(0, HEADS, full(3), after=finish)
+        sweep(0, MOST, full(3), after=finish)
+        sweep(MOST, HEADS, full(2) + full(3), after=finish)
 
     @pl.when(z < 3)
     def _():
+        when(z == 2, lambda: sweep(MOST, HEADS, full(2)))
+
         def body(h, _):
             finish(h)
             return 0
@@ -324,9 +340,9 @@
     for s in range(WINDOW):
         for j in range(2):
             if (s, j) != (WINDOW - 1, 0):
-                when((z >= s) & (z < slices - 1), lambda s=s, j=j: wait_half(ring_send.at[s, j]))
-    when(sends_back, lambda: wait_half(back_send.at[0]))
-    when(relays, lambda: wait_half(back_send.at[1]))
+                when((z >= s) & (z < slices - 1), lambda s=s, j=j: wait_ring(ring_send.at[s, j], s))
+    when(sends_back, lambda: wait_back(back_send.at[0]))
+    when(relays, lambda: wait_back(back_send.at[1]))
     wait_bytes(done.at[pl.ds(0, others)], out_send.at[0])
     wait_bytes(out, out_recv.at[0])
 
@@ -357,8 +373,8 @@
                 pltpu.VMEM((SLICE, QB), F32),
                 pltpu.VMEM((1, QB), F32),
                 pltpu.VMEM((HEADS, SLICE, DIM), BF16),
-                pltpu.VMEM((HALF, DIM), BF16),
-                pltpu.VMEM((DIM, HALF), BF16),
+                pltpu.VMEM((BACK, DIM), BF16),
+                pltpu.VMEM((DIM, BACK), BF16),
                 dma((1,)),
                 dma((HEADS,)),
                 dma((2,)),

time: 86.4 us -> 85.5 us (0.990)
  the two profiles are of different devices: /device:TPU:257 before, /device:TPU:129 now
where the time goes in v3:
time: 85.5 us; the launch traced here: 85.3 us
  Pallas kernels  82.2 us (96%)
  local copies, waits for them, and re-layouts  3.1 us (4%)
    pallas_call x1, Pallas kernels, local(): pl.pallas_call(functools.partial(kernel, slices), out_shape=jax.ShapeDtyp...  82.2 us
    unnamed x1, local copies, waits for them, and re-layouts  3.1 us

profile of v3, /device:TPU:129, one launch (start us, length us, event | category | flops | bytes accessed | tf_op | source)
XLA Modules:
  0.0 85.3 jit_solution(4421819168124806612)
XLA Ops:
  0.0 82.2 %shard_map.46 = bf16[128,8192]{1,0:T(8,128)(2,1)} custom-call(s32[1,8]{1,0:T(1,128)} %lengths.1, bf16[128,8192]{1,0:T(8,128)(2,1)} %bitcast.5, bf16[128,1024]{1,0:T(8,128)(2,1)} %bitcast.6, bf16[128,1024]{1,0:T(8,128)(2,1)} %bitcast.7), custom_call_target="tpu_custom_call" | custom-call | tf_op jit(solution)/shard_map/pallas_call | solution.py:357
  82.2 3.1 %copy.6 = bf16[1,128,8192]{2,1,0:T(8,128)(2,1)} copy(bf16[1,128,8192]{2,1,0:T(8,128)(2,1)} %bitcast.4) | data formatting | bytes 4194304

commit v4 on v3

--- a/solution.py
+++ b/solution.py
@@ -25,6 +25,7 @@
 EDGE = 256
 LOG2E_SCALE = 1.4426950408889634 * DIM**-0.5
 OFF = -1e30
+PIECES = 8
 
 
 def kernel(slices, lengths, q_in, k_in, v_in, out, qb, kb, vt, v_raw, v_turned, q_doc, k_doc,
@@ -345,6 +346,22 @@
     when(relays, lambda: wait_back(back_send.at[1]))
     wait_bytes(done.at[pl.ds(0, others)], out_send.at[0])
     wait_bytes(out, out_recv.at[0])
+
+
+def place(src, dst, held, load_sem, store_sem):
+    def copies(i):
+        rows = pl.ds(i * (TOK // PIECES), TOK // PIECES)
+        load = pltpu.make_async_copy(src.at[rows, :], held.at[rows, :], load_sem.at[i])
+        return load, pltpu.make_async_copy(held.at[rows, :], dst.at[rows, :], store_sem.at[i])
+
+    for i in range(PIECES):
+        copies(i)[0].start()
+    for i in range(PIECES):
+        load, store = copies(i)
+        load.wait()
+        store.start()
+    for i in range(PIECES):
+        copies(i)[1].wait()
 
 
 def solution(mesh):
@@ -390,7 +407,14 @@
             ],
             compiler_params=pltpu.CompilerParams(collective_id=0, has_side_effects=True, vmem_limit_bytes=56 * 2**20),
         )(lengths, query[0], key[0], value[0])
-        return attended[None]
+        return pl.pallas_call(
+            place,
+            out_shape=jax.ShapeDtypeStruct((rows, width), BF16),
+            in_specs=[hbm],
+            out_specs=hbm,
+            scratch_shapes=[pltpu.VMEM((rows, width), BF16), dma((PIECES,)), dma((PIECES,))],
+            compiler_params=pltpu.CompilerParams(vmem_limit_bytes=56 * 2**20),
+        )(attended)[None]
 
     placed = (P("rep", "head", None), P("rep", "head", None), P("rep", "head", None), P("rep", None))
     return jax.shard_map(local, mesh=mesh, in_specs=placed, out_specs=P("rep", "head", None), check_vma=False)

time: 85.5 us -> 84.9 us (level)
  local copies, waits for them, and re-layouts: 3.1 us -> 0 us
  Pallas kernels: 82.2 us -> 84.6 us
    unnamed x1 -> x0, local copies, waits for them, and re-layouts: 3.1 us -> none
    pallas_call x0 -> x1, Pallas kernels: none -> 2.39 us  [local(): pl.pallas_call(place, out_shape=jax.ShapeDtypeStruct((rows, width), BF16)...]
where the time goes in v4:
time: 84.9 us; the launch traced here: 84.8 us
  Pallas kernels  84.6 us (100%)
    pallas_call x1, Pallas kernels, local(): pl.pallas_call(functools.partial(kernel, slices), out_shape=jax.ShapeDtyp...  82.2 us
    pallas_call x1, Pallas kernels, local(): pl.pallas_call(place, out_shape=jax.ShapeDtypeStruct((rows, width), BF16)...  2.39 us

profile of v4, /device:TPU:129, one launch (start us, length us, event | category | flops | bytes accessed | tf_op | source)
XLA Modules:
  0.0 84.8 jit_solution(10656186369423785182)
XLA Ops:
  0.0 82.2 %shard_map.46.src = bf16[128,8192]{1,0:T(8,128)(2,1)} custom-call(s32[1,8]{1,0:T(1,128)} %lengths.1, bf16[128,8192]{1,0:T(8,128)(2,1)} %bitcast.4, bf16[128,1024]{1,0:T(8,128)(2,1)} %bitcast.5, bf16[128,1024]{1,0:T(8,128)(2,1)} %bitcast.6), custom_call_target="tpu_custom_call" | custom-call | tf_op jit(solution)/shard_map/pallas_call | solution.py:374
  82.2 2.4 %shard_map.47 = bf16[128,8192]{1,0:T(8,128)(2,1)} custom-call(bf16[128,8192]{1,0:T(8,128)(2,1)} %shard_map.46.src), custom_call_target="tpu_custom_call" | custom-call | tf_op jit(solution)/shard_map/pallas_call | solution.py:410
